TPU v7x, 32 devices: a whole 2x2x4 slice. The times are simulated.
32 devices in a mesh: pipe: 4 (over y, x), dp: 8 (over z, core).
Axes of the slice: x: 2, y: 2, z: 4, core: 2. Of those that a mesh axis runs over, the one named last changes fastest.
Arguments:
- new_input: bfloat16 [4, 1024, 8192], P('pipe', 'dp'), may hold values from -400 to 400
- new_gain: bfloat16 [4, 8192], P('pipe'), may hold values from 0.5 to 1.5
- queries: bfloat16 [4, 1024, 4096], P('pipe', 'dp'), may hold values from -5 to 5
- new_keys: bfloat16 [4, 1024, 512], P('pipe', 'dp'), may hold values from -5 to 5
- context_grad: bfloat16 [4, 1024, 4096], P('pipe', 'dp'), may hold values from -0.08984375 to 0.08984375
- segment_ids: int32 [4, 1024], P('pipe', 'dp'), may hold values from 0 to 15, never falling along the last dimension, each value on 1 to 128 neighbouring positions
- frozen_input: bfloat16 [4, 1024, 8192], P('pipe', 'dp'), may hold values from -400 to 400
- frozen_gain: bfloat16 [4, 8192], P('pipe'), may hold values from 0.5 to 1.5
- output_grad: bfloat16 [4, 1024, 8192], P('pipe', 'dp'), may hold values from -6 to 6
- kv_grad: bfloat16 [4, 1024, 1024], P('pipe', 'dp'), may hold values from -18 to 18
- kv_weight: bfloat16 [4, 8192, 1024], P('pipe', 'dp'), may hold values from -0.0625 to 0.0625
Outputs:
- cot_below: bfloat16 [4, 1024, 8192], P('pipe', 'dp')
- value_grad: float32 [4, 8192, 512], P('pipe', 'dp')
Inputs may be any that keep to these rules, and one draw needn't show every extreme that they name: `segment_ids`: within a section the numbers never fall; every number of 0 to 15 appears, on 1 to 128 positions in a row, one on exactly 128.
All inputs are finite; a program needn't handle non-finite values.
Results may differ from a plain program's by a relative error of at most 0.0056.
Values may be sent and summed in bfloat16 or wider, within the bound.
No kernel may reach another device: no remote copies, remote signals or barrier semaphores. Data moves between devices by JAX's collectives and lax.ppermute only.
A program may use at most 128 MiB of HBM per device.

v0:
```python
import functools
import math

import jax
import jax.numpy as jnp
from jax import lax
from jax.experimental import pallas as pl
from jax.experimental.pallas import tpu as pltpu
from jax.sharding import PartitionSpec as P

HEAD = 128
CORES = 2
MIB = 1 << 20

norm_eps = 1e-05
masked_value = -1e30

whole = pl.BlockSpec(memory_space=pl.ANY)
scalars = pl.BlockSpec(memory_space=pltpu.SMEM)


def from_behind(array, axis, by):
    length = lax.axis_size(axis)
    pairs = [(i, i + by) for i in range(length) if 0 <= i + by < length]
    return lax.ppermute(array, axis, pairs)


def along_chips(array, by):
    length = lax.axis_size("dp")
    return lax.ppermute(array, "dp", [(i, (i + by * CORES) % length) for i in range(length)])


def swap_cores(array):
    length = lax.axis_size("dp")
    return lax.ppermute(array, "dp", [(i, i ^ 1) for i in range(length)])


def call(body, name, flops, nbytes, vmem=24, **kwargs):
    return pl.pallas_call(
        body,
        name=name,
        compiler_params=pltpu.CompilerParams(vmem_limit_bytes=vmem * MIB),
        cost_estimate=pl.CostEstimate(flops=flops, bytes_accessed=nbytes, transcendentals=0),
        **kwargs,
    )


def part_columns(chip, half, core, width):
    owner = chip * CORES + (core if half == 0 else CORES - 1 - core)
    return pl.ds(pl.multiple_of(owner * width, width), width)


def norm_kernel(chips, ahead, place_ref, x_ref, gain_ref, cot_ref, *rest):
    out_refs = rest[-len(ahead):]
    chip, core = place_ref[0], place_ref[1]
    values = x_ref[...].astype(jnp.float32)
    inverse = lax.rsqrt(jnp.mean(values * values, axis=-1, keepdims=True) + norm_eps)
    front = cot_ref.shape[1]
    width = (out_refs[0].shape[1] - front) // CORES
    for by, out_ref in zip(ahead, out_refs):
        to = lax.rem(chip + by, chips)
        out_ref[:, :front] = cot_ref[...]
        for half in range(CORES):
            cols = part_columns(to, half, core, width)
            out_ref[:, front + half * width:front + (half + 1) * width] = (
                x_ref[:, cols].astype(jnp.float32) * inverse * gain_ref[:, cols].astype(jnp.float32)
            ).astype(out_ref.dtype)


def normalize(place, rows, gain, cot, chips, ahead, after):
    tokens, width = rows.shape
    front = cot.shape[1]
    block = min(tokens, 32)
    out_width = front + width // chips
    return call(
        functools.partial(norm_kernel, chips, ahead), "norm_forward",
        4 * tokens * width, 2 * tokens * width + 2 * tokens * out_width * len(ahead),
        grid=(tokens // block,),
        in_specs=[
            scalars,
            pl.BlockSpec((block, width), lambda i: (i, 0)),
            pl.BlockSpec((1, width), lambda i: (0, 0)),
            pl.BlockSpec((block, front), lambda i: (i, 0)),
        ] + [whole] * len(after),
        out_specs=[pl.BlockSpec((block, out_width), lambda i: (i, 0))] * len(ahead),
        out_shape=[jax.ShapeDtypeStruct((tokens, out_width), jnp.bfloat16)] * len(ahead),
    )(place, rows, gain, cot, *after)


def attend_kernel(query_ref, key_ref, grad_ref, row_seg_ref, col_seg_ref, out_ref):
    tokens = key_ref.shape[0]
    group = query_ref.shape[1] // HEAD
    at_query = lax.broadcasted_iota(jnp.int32, (tokens, tokens), 0)
    at_key = lax.broadcasted_iota(jnp.int32, (tokens, tokens), 1)
    visible = (col_seg_ref[...] == row_seg_ref[...]) & (at_key <= at_query)
    keys = key_ref[...]
    total = jnp.zeros((tokens, HEAD), jnp.float32)
    for head in range(group):
        cols = slice(head * HEAD, (head + 1) * HEAD)
        scores = lax.dot_general(
            query_ref[:, cols], keys, (((1,), (1,)), ((), ())),
            preferred_element_type=jnp.float32,
        ) / math.sqrt(HEAD)
        masked = jnp.where(visible, scores, masked_value)
        highest = jnp.max(masked, axis=-1, keepdims=True)
        weights = jnp.where(visible, jnp.exp(masked - highest), 0.0)
        attention = (weights / jnp.sum(weights, axis=-1, keepdims=True)).astype(jnp.bfloat16)
        total += lax.dot_general(
            attention, grad_ref[:, cols], (((0,), (0,)), ((), ())),
            preferred_element_type=jnp.float32,
        )
    out_ref[...] = total.astype(out_ref.dtype)


def attend(queries, keys, grads, segments):
    tokens, kv_width = keys.shape
    heads = kv_width // HEAD
    wide = queries.shape[1] // heads
    return call(
        attend_kernel, "attend",
        4 * tokens * tokens * queries.shape[1], 4 * tokens * queries.shape[1],
        grid=(heads,),
        in_specs=[
            pl.BlockSpec((tokens, wide), lambda i: (0, i)),
            pl.BlockSpec((tokens, HEAD), lambda i: (0, i)),
            pl.BlockSpec((tokens, wide), lambda i: (0, i)),
            pl.BlockSpec((1, tokens), lambda i: (0, 0)),
            pl.BlockSpec((tokens, 1), lambda i: (0, 0)),
        ],
        out_specs=pl.BlockSpec((tokens, HEAD), lambda i: (0, i)),
        out_shape=jax.ShapeDtypeStruct((tokens, kv_width), jnp.bfloat16),
    )(queries, keys, grads, segments, segments.reshape(tokens, 1))


def project_kernel(chips, steps, own_ref, other_ref, *rest):
    row_refs, out_refs, gathered = rest[:chips], rest[-chips - 1:-1], rest[-1]
    taken, depth = row_refs[0].shape
    step = pl.program_id(0)

    @pl.when(step == 0)
    def _():
        for by in range(chips):
            gathered[by] = row_refs[by][...]

    def multiply(weight_ref):
        product = lax.dot_general(
            gathered[...].reshape(chips * taken, depth), weight_ref[...], (((1,), (1,)), ((), ())),
            preferred_element_type=jnp.float32,
        ).astype(jnp.bfloat16)
        for by in range(chips):
            out_refs[by][...] = product[by * taken:(by + 1) * taken]

    @pl.when(step < steps)
    def _():
        multiply(own_ref)

    @pl.when(step >= steps)
    def _():
        multiply(other_ref)


def project(rows, own, other, after):
    chips = len(rows)
    taken, depth = rows[0].shape
    width = own.shape[0]
    block = min(width, 256)
    steps = width // block
    return call(
        functools.partial(project_kernel, chips, steps), "project",
        4 * chips * taken * depth * width, 2 * (chips * taken * (depth + 2 * width) + 2 * width * depth),
        grid=(CORES * steps,),
        in_specs=[
            pl.BlockSpec((block, depth), lambda i: (jnp.minimum(i, steps - 1), 0)),
            pl.BlockSpec((block, depth), lambda i: (jnp.maximum(i - steps, 0), 0)),
        ] + [pl.BlockSpec((taken, depth), lambda i: (0, 0))] * chips + [whole] * len(after),
        out_specs=[pl.BlockSpec((taken, block), lambda i: (0, i))] * chips,
        out_shape=[jax.ShapeDtypeStruct((taken, CORES * width), jnp.bfloat16)] * chips,
        scratch_shapes=[pltpu.VMEM((chips, taken, depth), jnp.bfloat16)],
    )(own, other, *rows, *after)


def backward_kernel(chips, place_ref, x_ref, gain_ref, grad_ref, *rest):
    cot_refs, out_ref = rest[:chips], rest[-1]
    chip, core = place_ref[0], place_ref[1]
    values = x_ref[...].astype(jnp.float32)
    width = cot_refs[0].shape[1] // CORES
    inverse = lax.rsqrt(jnp.mean(values * values, axis=-1, keepdims=True) + norm_eps)
    inner = jnp.zeros_like(inverse)

    def parts():
        for by, cot_ref in enumerate(cot_refs):
            source = lax.rem(chip + chips - by, chips)
            for half in range(CORES):
                cols = part_columns(source, half, core, width)
                cot = cot_ref[:, half * width:(half + 1) * width].astype(jnp.float32)
                yield cols, gain_ref[:, cols].astype(jnp.float32) * cot

    for cols, scaled in parts():
        inner += jnp.sum(x_ref[:, cols].astype(jnp.float32) * scaled, axis=-1, keepdims=True)
    factor = inverse * inverse * inverse * (inner / x_ref.shape[1])
    for cols, scaled in parts():
        out_ref[:, cols] = (
            grad_ref[:, cols].astype(jnp.float32)
            + inverse * scaled
            - x_ref[:, cols].astype(jnp.float32) * factor
        ).astype(out_ref.dtype)


def norm_backward(place, cots, rows, gain, grads, after):
    tokens, width = rows.shape
    taken, part_width = cots[0].shape
    block = min(taken, 32)
    return call(
        functools.partial(backward_kernel, len(cots)), "norm_backward",
        10 * taken * width, 8 * taken * width,
        grid=(taken // block,),
        in_specs=[
            scalars,
            pl.BlockSpec((block, width), lambda i: (i, 0)),
            pl.BlockSpec((1, width), lambda i: (0, 0)),
            pl.BlockSpec((block, width), lambda i: (i, 0)),
        ] + [pl.BlockSpec((block, part_width), lambda i: (i, 0))] * len(cots) + [whole] * len(after),
        out_specs=pl.BlockSpec((block, width), lambda i: (i, 0)),
        out_shape=jax.ShapeDtypeStruct((taken, width), jnp.bfloat16),
    )(place, rows, gain, grads, *cots, *after)


def outer_kernel(arrays, sums, *refs):
    cots, columns, terms = refs[:arrays], refs[arrays:2 * arrays], refs[2 * arrays:2 * arrays + sums]
    total = None
    for cot_ref, column_ref in zip(cots, columns):
        product = lax.dot_general(
            column_ref[...], cot_ref[...], (((0,), (0,)), ((), ())),
            preferred_element_type=jnp.float32,
        )
        total = product if total is None else total + product
    for term in terms:
        total += term[...].astype(jnp.float32)
    refs[-1][...] = total.astype(refs[-1].dtype)


def outer(payloads, cot_width, half, before, dtype, after):
    tokens, wide = payloads[0].shape
    width = (wide - cot_width) // CORES
    block = math.gcd(math.gcd(width, 256), cot_width)
    first = (cot_width + half * width) // block
    out_spec = pl.BlockSpec((block, cot_width), lambda i: (i, 0))
    arrays = len(payloads)
    return call(
        functools.partial(outer_kernel, arrays, len(before)), "outer",
        2 * arrays * tokens * width * cot_width, 2 * arrays * tokens * width + 4 * width * cot_width,
        grid=(width // block,),
        in_specs=[pl.BlockSpec((tokens, cot_width), lambda i: (0, 0))] * arrays
        + [pl.BlockSpec((tokens, block), lambda i: (0, first + i))] * arrays
        + [out_spec] * len(before) + [whole] * len(after),
        out_specs=out_spec,
        out_shape=jax.ShapeDtypeStruct((width, cot_width), dtype),
    )(*payloads, *payloads, *before, *after)


def shards(
    new_input,
    new_gain,
    queries,
    new_keys,
    context_grad,
    segment_ids,
    frozen_input,
    frozen_gain,
    output_grad,
    kv_grad,
    kv_weight,
):
    chips = lax.axis_size("dp") // CORES
    kv_width = new_keys.shape[2]
    at = lax.axis_index("dp")
    place = jnp.stack([at // CORES, at % CORES]).astype(jnp.int32)
    middle = chips // 2
    order = [by for by in range(1, chips) if by != middle] + [middle]
    first, later = order[:1], order[1:]

    rows = [kv_grad[0]] + [along_chips(kv_grad[0], chips - by) for by in range(1, chips)]
    other_weight = swap_cores(kv_weight[0])
    value_cot = attend(queries[0], new_keys[0], context_grad[0], segment_ids)

    after = [rows[by] for by in order[:-1]]
    early = normalize(place, new_input[0], new_gain, value_cot, chips, [0] + first, after)
    columns = [early[0]] + [along_chips(block, by) for block, by in zip(early[1:], first)]

    parts = project(rows, kv_weight[0], other_weight, early[:1])
    arrived = [parts[0]] + [along_chips(parts[by], by) for by in range(1, chips)]

    after = [arrived[by] for by in order[:-1]]
    late = normalize(place, new_input[0], new_gain, value_cot, chips, later, after)
    columns += [along_chips(block, by) for block, by in zip(late, later)]

    input_cot = norm_backward(place, arrived, frozen_input[0], frozen_gain, output_grad[0], [late[0]] + columns[1:1 + len(first)])
    cot_below = from_behind(input_cot, "pipe", -1)

    sums = [outer(columns[:-1], kv_width, half, [], jnp.float32, []) for half in range(CORES)]
    given = outer(columns[-1:], kv_width, 1, [sums[1]], jnp.bfloat16, [cot_below])
    taken = swap_cores(given)
    grad = outer(columns[-1:], kv_width, 0, [sums[0], taken], jnp.float32, [])
    return (cot_below[None], grad[None])


def solution(mesh):
    placed = (
        P("pipe", "dp", None),
        P("pipe", None),
        P("pipe", "dp", None),
        P("pipe", "dp", None),
        P("pipe", "dp", None),
        P("pipe", "dp"),
        P("pipe", "dp", None),
        P("pipe", None),
        P("pipe", "dp", None),
        P("pipe", "dp", None),
        P("pipe", "dp", None),
    )
    return jax.shard_map(
        shards,
        mesh=mesh,
        in_specs=placed,
        out_specs=(P("pipe", "dp", None), P("pipe", "dp", None)),
        check_vma=False,
    )
```

profile of v0, /device:TPU:0, one launch (start us, length us, event | category | flops | bytes accessed | tf_op | source)
XLA Modules:
  0.0 156.5 jit_solution(17391169125965736009)
XLA Ops:
  0.6 0.0 copy-start
  0.6 0.5 collective-permute-start
  1.2 2.6 %collective-permute-start.3 = (bf16[128,1024]{1,0:T(8,128)(2,1)}, bf16[128,1024]{1,0:T(8,128)(2,1)S(1)}, u32[]{:S(2)}, u32[]{:S(2)}) collective-permute-start(bf16[128,1024]{1,0:T(8,128)(2,1)} %bitcast.24), channel_id=1, source_target_pairs={{0,2},{1,3},{2,4},{3,5},{4,6},{5,7},{6,0},{7,1},{8,10},{9,11},{10,... | collective-permute-start | bytes 786440 | tf_op jit(solution)/shard_map/ppermute | solution.py:30
  3.8 2.1 %collective-permute-start.1 = (bf16[128,1024]{1,0:T(8,128)(2,1)}, bf16[128,1024]{1,0:T(8,128)(2,1)S(1)}, u32[]{:S(2)}, u32[]{:S(2)}) collective-permute-start(bf16[128,1024]{1,0:T(8,128)(2,1)} %bitcast.25), channel_id=1, source_target_pairs={{0,6},{1,7},{2,0},{3,1},{4,2},{5,3},{6,4},{7,5},{8,14},{9,15},{10,... | collective-permute-start | bytes 786440 | tf_op jit(solution)/shard_map/ppermute | solution.py:30
  5.9 0.9 collective-permute-start.2
  6.8 0.8 copy.13.col_seg_ref
  7.6 0.0 copy-start.3
  7.6 1.2 copy-done.3
  8.8 1.2 copy-done.4
  10.1 0.9 copy-done.6
  11.0 0.7 copy-done.8
  11.6 4.5 %attend.1.cot_ref = bf16[128,512]{1,0:T(8,128)(2,1)S(1)} custom-call(bf16[128,4096]{1,0:T(8,128)(2,1)S(1)} %bitcast.18, bf16[128,512]{1,0:T(8,128)(2,1)S(1)} %bitcast.20, bf16[128,4096]{1,0:T(8,128)(2,1)S(1)} %bitcast.19, s32[1,128]{1,0:T(1,128)S(1)} %copy-done.8, s32[128,1]{1,0:T(8,128)S(1)} %copy.13.col_seg_ref), custom_call_target="tpu_custom_call" | custom-call | flops 268435456 | bytes 2097152 | tf_op jit(solution)/shard_map/attend/pallas_call | solution.py:119
  16.1 0.1 pad_add_fusion.place_ref
  16.2 0.0 collective-permute-done.3.rest_1_.rest_3_
  16.2 1.8 %collective-permute-done.1.rest_0_.rest_1_ = bf16[128,1024]{1,0:T(8,128)(2,1)S(1)} collective-permute-done((bf16[128,1024]{1,0:T(8,128)(2,1)}, bf16[128,1024]{1,0:T(8,128)(2,1)S(1)}, u32[]{:S(2)}, u32[]{:S(2)}) %collective-permute-start.1) | collective-permute-done | bytes 262176 | tf_op jit(solution)/shard_map/ppermute | solution.py:30
  18.0 0.0 copy-done
  18.0 0.0 copy-done.5
  18.0 1.5 norm_forward.2
  19.6 5.3 %collective-permute-start.7 = (bf16[128,2560]{1,0:T(8,128)(2,1)S(1)}, bf16[128,2560]{1,0:T(8,128)(2,1)S(1)}, u32[]{:S(2)}, u32[]{:S(2)}) collective-permute-start(bf16[128,2560]{1,0:T(8,128)(2,1)S(1)} %get-tuple-element.16), channel_id=1, source_target_pairs={{0,2},{1,3},{2,4},{3,5},{4,6},{5,7},{6,0},{7,1},{8,10},{9,11},{10,... | collective-permute-start | bytes 1966088 | tf_op jit(solution)/shard_map/ppermute | solution.py:30
  24.8 19.0 %collective-permute-done.2.rest_2_ = bf16[128,1024]{1,0:T(8,128)(2,1)S(1)} collective-permute-done((bf16[128,1024]{1,0:T(8,128)(2,1)}, bf16[128,1024]{1,0:T(8,128)(2,1)S(1)}, u32[]{:S(2)}, u32[]{:S(2)}) %collective-permute-start.2) | collective-permute-done | bytes 262176 | tf_op jit(solution)/shard_map/ppermute | solution.py:30
  43.8 0.0 collective-permute-done.other_ref
  43.8 0.0 copy-done.9
  43.9 0.0 copy-start.2
  43.9 6.5 %project.1 = (bf16[128,2048]{1,0:T(8,128)(2,1)S(1)}, bf16[128,2048]{1,0:T(8,128)(2,1)S(1)}, bf16[128,2048]{1,0:T(8,128)(2,1)S(1)}, bf16[128,2048]{1,0:T(8,128)(2,1)S(1)}) custom-call(bf16[1024,1024]{1,0:T(8,128)(2,1)S(1)} %bitcast.23, bf16[1024,1024]{1,0:T(8,128)(2,1)} %collective-permute-done.other_ref, bf16[128,1024]{1,0:T(8,128)(2,1)S(1)} %bitcast.27, ...), custom_call_target="tpu_custom_call" | custom-call | flops 2147483648 | bytes 7340032 | tf_op jit(solution)/shard_map/project/pallas_call | solution.py:168
  50.4 0.0 copy-start.1
  50.4 0.0 copy-start.7
  50.4 0.1 collective-permute-start.4
  50.5 3.8 %collective-permute-start.6 = (bf16[128,2048]{1,0:T(8,128)(2,1)S(1)}, bf16[128,2048]{1,0:T(8,128)(2,1)S(1)}, u32[]{:S(2)}, u32[]{:S(2)}) collective-permute-start(bf16[128,2048]{1,0:T(8,128)(2,1)S(1)} %get-tuple-element.14), channel_id=1, source_target_pairs={{0,6},{1,7},{2,0},{3,1},{4,2},{5,3},{6,4},{7,5},{8,14},{9,15},{10,... | collective-permute-start | bytes 1572872 | tf_op jit(solution)/shard_map/ppermute | solution.py:30
  54.3 0.0 collective-permute-start.5
  54.3 12.8 %collective-permute-done.4.rest_0_.rest_1_ = bf16[128,2048]{1,0:T(8,128)(2,1)S(1)} collective-permute-done((bf16[128,2048]{1,0:T(8,128)(2,1)S(1)}, bf16[128,2048]{1,0:T(8,128)(2,1)S(1)}, u32[]{:S(2)}, u32[]{:S(2)}) %collective-permute-start.4) | collective-permute-done | bytes 524320 | tf_op jit(solution)/shard_map/ppermute | solution.py:30
  67.1 10.8 %collective-permute-done.6.rest_1_.rest_3_ = bf16[128,2048]{1,0:T(8,128)(2,1)S(1)} collective-permute-done((bf16[128,2048]{1,0:T(8,128)(2,1)S(1)}, bf16[128,2048]{1,0:T(8,128)(2,1)S(1)}, u32[]{:S(2)}, u32[]{:S(2)}) %collective-permute-start.6) | collective-permute-done | bytes 524320 | tf_op jit(solution)/shard_map/ppermute | solution.py:30
  77.9 1.5 norm_forward.3
  79.5 0.0 collective-permute-done.7.rest_5_.refs_1_.refs_4_
  79.5 17.9 %collective-permute-done.5.rest_2_ = bf16[128,2048]{1,0:T(8,128)(2,1)S(1)} collective-permute-done((bf16[128,2048]{1,0:T(8,128)(2,1)S(1)}, bf16[128,2048]{1,0:T(8,128)(2,1)S(1)}, u32[]{:S(2)}, u32[]{:S(2)}) %collective-permute-start.5) | collective-permute-done | bytes 524320 | tf_op jit(solution)/shard_map/ppermute | solution.py:30
  97.4 3.3 %norm_backward.1 = bf16[128,8192]{1,0:T(8,128)(2,1)S(1)} custom-call(s32[2]{0:T(128)S(1)} %pad_add_fusion.place_ref, bf16[128,8192]{1,0:T(8,128)(2,1)S(1)} %bitcast.16, bf16[1,8192]{1,0:T(2,128)(2,1)S(1)} %copy-done.7, bf16[128,8192]{1,0:T(8,128)(2,1)S(1)} %bitcast.17, bf16[128,2048]{1,0:T(8,128)(2,1)S(1)} %get-tuple-element.11.rest_0_, ...), custom_call_target="tpu_custom_call" | custom-call | flops 10485760 | bytes 8388608 | tf_op jit(solution)/shard_map/norm_backward/pallas_call | solution.py:213
  100.7 1.3 collective-permute-start.8
  102.0 1.2 collective-permute-start.10
  103.2 0.0 collective-permute-start.9
  103.2 16.1 %collective-permute-done.10.refs_2_.refs_5_ = bf16[128,2560]{1,0:T(8,128)(2,1)S(1)} collective-permute-done((bf16[128,2560]{1,0:T(8,128)(2,1)S(1)}, bf16[128,2560]{1,0:T(8,128)(2,1)S(1)}, u32[]{:S(2)}, u32[]{:S(2)}) %collective-permute-start.10) | collective-permute-done | bytes 655392 | tf_op jit(solution)/shard_map/ppermute | solution.py:30
  119.3 1.7 %outer.5.refs_2_ = f32[1024,512]{1,0:T(8,128)S(1)} custom-call(bf16[128,2560]{1,0:T(8,128)(2,1)S(1)} %get-tuple-element.10.rest_4_.refs_0_.refs_3_, bf16[128,2560]{1,0:T(8,128)(2,1)S(1)} %collective-permute-done.7.rest_5_.refs_1_.refs_4_, bf16[128,2560]{1,0:T(8,128)(2,1)S(1)} %collective-permute-done.10.refs_2_.refs_5_, ...), custom_call_target="tpu_custom_call" | custom-call | flops 402653184 | bytes 2883584 | tf_op jit(solution)/shard_map/outer/pallas_call | solution.py:249
  121.1 22.6 %collective-permute-done.9.refs_0_.refs_1_ = bf16[128,2560]{1,0:T(8,128)(2,1)S(1)} collective-permute-done((bf16[128,2560]{1,0:T(8,128)(2,1)S(1)}, bf16[128,2560]{1,0:T(8,128)(2,1)S(1)}, u32[]{:S(2)}, u32[]{:S(2)}) %collective-permute-start.9) | collective-permute-done | bytes 655392 | tf_op jit(solution)/shard_map/ppermute | solution.py:30
  143.7 5.2 %collective-permute-done.8.refs_3_ = bf16[128,8192]{1,0:T(8,128)(2,1)S(1)} collective-permute-done((bf16[128,8192]{1,0:T(8,128)(2,1)S(1)}, bf16[128,8192]{1,0:T(8,128)(2,1)S(1)}, u32[]{:S(2)}, u32[]{:S(2)}) %collective-permute-start.8) | collective-permute-done | bytes 2097184 | tf_op jit(solution)/shard_map/ppermute | solution.py:25
  149.0 1.1 outer.6
  150.1 0.1 collective-permute-start.11
  150.1 1.8 %outer.4.refs_2_ = f32[1024,512]{1,0:T(8,128)S(1)} custom-call(bf16[128,2560]{1,0:T(8,128)(2,1)S(1)} %get-tuple-element.10.rest_4_.refs_0_.refs_3_, bf16[128,2560]{1,0:T(8,128)(2,1)S(1)} %collective-permute-done.7.rest_5_.refs_1_.refs_4_, bf16[128,2560]{1,0:T(8,128)(2,1)S(1)} %collective-permute-done.10.refs_2_.refs_5_, ...), custom_call_target="tpu_custom_call" | custom-call | flops 402653184 | bytes 2883584 | tf_op jit(solution)/shard_map/outer/pallas_call | solution.py:249
  151.9 0.9 collective-permute-done.11.refs_3_
  152.8 2.4 %outer.7 = f32[1024,512]{1,0:T(8,128)} custom-call(bf16[128,2560]{1,0:T(8,128)(2,1)S(1)} %collective-permute-done.9.refs_0_.refs_1_, bf16[128,2560]{1,0:T(8,128)(2,1)S(1)} %collective-permute-done.9.refs_0_.refs_1_, f32[1024,512]{1,0:T(8,128)S(1)} %outer.4.refs_2_, bf16[1024,512]{1,0:T(8,128)(2,1)S(1)} %collective-permute-done.11.refs_3_), custom_call_target="tpu_custom_call" | custom-call | flops 134217728 | bytes 2359296 | tf_op jit(solution)/shard_map/outer/pallas_call | solution.py:249
  155.2 1.3 copy.15
  (10 shorter events, 0.0 us)
Async XLA Ops:
  0.6 17.4 %copy-start = (bf16[1,128,8192]{2,1,0:T(8,128)(2,1)S(1)}, bf16[1,128,8192]{2,1,0:T(8,128)(2,1)}, u32[]{:S(2)}) copy-start(bf16[1,128,8192]{2,1,0:T(8,128)(2,1)} %param.11) | copy-start | bytes 6291460
  0.6 43.2 %collective-permute-start = (bf16[1024,1024]{1,0:T(8,128)(2,1)}, bf16[1024,1024]{1,0:T(8,128)(2,1)}, u32[]{:S(2)}, u32[]{:S(2)}) collective-permute-start(bf16[1024,1024]{1,0:T(8,128)(2,1)} %bitcast.22), channel_id=1, source_target_pairs={{0,1},{1,0},{2,3},{3,2},{4,5},{5,4},{6,7},{7,6},{8,9},{9,8},{10,11... | collective-permute-start | bytes 6291464 | tf_op jit(solution)/shard_map/ppermute | solution.py:35
  1.2 15.0 %collective-permute-start.3 = (bf16[128,1024]{1,0:T(8,128)(2,1)}, bf16[128,1024]{1,0:T(8,128)(2,1)S(1)}, u32[]{:S(2)}, u32[]{:S(2)}) collective-permute-start(bf16[128,1024]{1,0:T(8,128)(2,1)} %bitcast.24), channel_id=1, source_target_pairs={{0,2},{1,3},{2,4},{3,5},{4,6},{5,7},{6,0},{7,1},{8,10},{9,11},{10,... | collective-permute-start | bytes 786440 | tf_op jit(solution)/shard_map/ppermute | solution.py:30
  3.8 14.2 %collective-permute-start.1 = (bf16[128,1024]{1,0:T(8,128)(2,1)}, bf16[128,1024]{1,0:T(8,128)(2,1)S(1)}, u32[]{:S(2)}, u32[]{:S(2)}) collective-permute-start(bf16[128,1024]{1,0:T(8,128)(2,1)} %bitcast.25), channel_id=1, source_target_pairs={{0,6},{1,7},{2,0},{3,1},{4,2},{5,3},{6,4},{7,5},{8,14},{9,15},{10,... | collective-permute-start | bytes 786440 | tf_op jit(solution)/shard_map/ppermute | solution.py:30
  5.9 37.9 %collective-permute-start.2 = (bf16[128,1024]{1,0:T(8,128)(2,1)}, bf16[128,1024]{1,0:T(8,128)(2,1)S(1)}, u32[]{:S(2)}, u32[]{:S(2)}) collective-permute-start(bf16[128,1024]{1,0:T(8,128)(2,1)} %bitcast.26), channel_id=1, source_target_pairs={{0,4},{1,5},{2,6},{3,7},{4,0},{5,1},{6,2},{7,3},{8,12},{9,13},{10,... | collective-permute-start | bytes 786440 | tf_op jit(solution)/shard_map/ppermute | solution.py:30
  7.6 1.2 copy-start.3
  8.8 1.2 copy-start.4
  10.1 0.9 copy-start.6
  11.0 0.7 copy-start.8
  11.6 6.4 %copy-start.5 = (bf16[1,8192]{1,0:T(2,128)(2,1)S(1)}, bf16[1,8192]{1,0:T(2,128)(2,1)}, u32[]{:S(2)}) copy-start(bf16[1,8192]{1,0:T(2,128)(2,1)} %gain_ref.4) | copy-start | bytes 49156
  11.6 32.2 %copy-start.9 = (bf16[1,1024,1024]{2,1,0:T(8,128)(2,1)S(1)}, bf16[1,1024,1024]{2,1,0:T(8,128)(2,1)}, u32[]{:S(2)}) copy-start(bf16[1,1024,1024]{2,1,0:T(8,128)(2,1)} %param.21) | copy-start | bytes 6291460
  11.6 32.2 %copy-start.10 = (bf16[1,128,1024]{2,1,0:T(8,128)(2,1)S(1)}, bf16[1,128,1024]{2,1,0:T(8,128)(2,1)}, u32[]{:S(2)}) copy-start(bf16[1,128,1024]{2,1,0:T(8,128)(2,1)} %param.20) | copy-start | bytes 786436
  19.6 59.9 %collective-permute-start.7 = (bf16[128,2560]{1,0:T(8,128)(2,1)S(1)}, bf16[128,2560]{1,0:T(8,128)(2,1)S(1)}, u32[]{:S(2)}, u32[]{:S(2)}) collective-permute-start(bf16[128,2560]{1,0:T(8,128)(2,1)S(1)} %get-tuple-element.16), channel_id=1, source_target_pairs={{0,2},{1,3},{2,4},{3,5},{4,6},{5,7},{6,0},{7,1},{8,10},{9,11},{10,... | collective-permute-start | bytes 1966088 | tf_op jit(solution)/shard_map/ppermute | solution.py:30
  43.9 53.6 %copy-start.2 = (bf16[1,128,8192]{2,1,0:T(8,128)(2,1)S(1)}, bf16[1,128,8192]{2,1,0:T(8,128)(2,1)}, u32[]{:S(2)}) copy-start(bf16[1,128,8192]{2,1,0:T(8,128)(2,1)} %param.19) | copy-start | bytes 6291460
  50.4 47.0 %copy-start.1 = (bf16[1,128,8192]{2,1,0:T(8,128)(2,1)S(1)}, bf16[1,128,8192]{2,1,0:T(8,128)(2,1)}, u32[]{:S(2)}) copy-start(bf16[1,128,8192]{2,1,0:T(8,128)(2,1)} %param.17) | copy-start | bytes 6291460
  50.4 47.0 %copy-start.7 = (bf16[1,8192]{1,0:T(2,128)(2,1)S(1)}, bf16[1,8192]{1,0:T(2,128)(2,1)}, u32[]{:S(2)}) copy-start(bf16[1,8192]{1,0:T(2,128)(2,1)} %gain_ref.5) | copy-start | bytes 49156
  50.4 16.7 %collective-permute-start.4 = (bf16[128,2048]{1,0:T(8,128)(2,1)S(1)}, bf16[128,2048]{1,0:T(8,128)(2,1)S(1)}, u32[]{:S(2)}, u32[]{:S(2)}) collective-permute-start(bf16[128,2048]{1,0:T(8,128)(2,1)S(1)} %get-tuple-element.12), channel_id=1, source_target_pairs={{0,2},{1,3},{2,4},{3,5},{4,6},{5,7},{6,0},{7,1},{8,10},{9,11},{10,... | collective-permute-start | bytes 1572872 | tf_op jit(solution)/shard_map/ppermute | solution.py:30
  50.5 27.5 %collective-permute-start.6 = (bf16[128,2048]{1,0:T(8,128)(2,1)S(1)}, bf16[128,2048]{1,0:T(8,128)(2,1)S(1)}, u32[]{:S(2)}, u32[]{:S(2)}) collective-permute-start(bf16[128,2048]{1,0:T(8,128)(2,1)S(1)} %get-tuple-element.14), channel_id=1, source_target_pairs={{0,6},{1,7},{2,0},{3,1},{4,2},{5,3},{6,4},{7,5},{8,14},{9,15},{10,... | collective-permute-start | bytes 1572872 | tf_op jit(solution)/shard_map/ppermute | solution.py:30
  54.3 43.1 %collective-permute-start.5 = (bf16[128,2048]{1,0:T(8,128)(2,1)S(1)}, bf16[128,2048]{1,0:T(8,128)(2,1)S(1)}, u32[]{:S(2)}, u32[]{:S(2)}) collective-permute-start(bf16[128,2048]{1,0:T(8,128)(2,1)S(1)} %get-tuple-element.13), channel_id=1, source_target_pairs={{0,4},{1,5},{2,6},{3,7},{4,0},{5,1},{6,2},{7,3},{8,12},{9,13},{10,... | collective-permute-start | bytes 1572872 | tf_op jit(solution)/shard_map/ppermute | solution.py:30
  100.7 48.3 %collective-permute-start.8 = (bf16[128,8192]{1,0:T(8,128)(2,1)S(1)}, bf16[128,8192]{1,0:T(8,128)(2,1)S(1)}, u32[]{:S(2)}, u32[]{:S(2)}) collective-permute-start(bf16[128,8192]{1,0:T(8,128)(2,1)S(1)} %norm_backward.1), channel_id=1, source_target_pairs={{8,0},{16,8},{24,16},{9,1},{17,9},{25,17},{10,2},{18,10},{26,18},{... | collective-permute-start | bytes 6291464 | tf_op jit(solution)/shard_map/ppermute | solution.py:25
  102.0 17.4 %collective-permute-start.10 = (bf16[128,2560]{1,0:T(8,128)(2,1)S(1)}, bf16[128,2560]{1,0:T(8,128)(2,1)S(1)}, u32[]{:S(2)}, u32[]{:S(2)}) collective-permute-start(bf16[128,2560]{1,0:T(8,128)(2,1)S(1)} %get-tuple-element.15.rest_4_), channel_id=1, source_target_pairs={{0,6},{1,7},{2,0},{3,1},{4,2},{5,3},{6,4},{7,5},{8,14},{9,15},{10,... | collective-permute-start | bytes 1966088 | tf_op jit(solution)/shard_map/ppermute | solution.py:30
  103.2 40.5 %collective-permute-start.9 = (bf16[128,2560]{1,0:T(8,128)(2,1)S(1)}, bf16[128,2560]{1,0:T(8,128)(2,1)S(1)}, u32[]{:S(2)}, u32[]{:S(2)}) collective-permute-start(bf16[128,2560]{1,0:T(8,128)(2,1)S(1)} %get-tuple-element.17), channel_id=1, source_target_pairs={{0,4},{1,5},{2,6},{3,7},{4,0},{5,1},{6,2},{7,3},{8,12},{9,13},{10,... | collective-permute-start | bytes 1966088 | tf_op jit(solution)/shard_map/ppermute | solution.py:30
  150.1 2.7 %collective-permute-start.11 = (bf16[1024,512]{1,0:T(8,128)(2,1)S(1)}, bf16[1024,512]{1,0:T(8,128)(2,1)S(1)}, u32[]{:S(2)}, u32[]{:S(2)}) collective-permute-start(bf16[1024,512]{1,0:T(8,128)(2,1)S(1)} %outer.6), channel_id=1, source_target_pairs={{0,1},{1,0},{2,3},{3,2},{4,5},{5,4},{6,7},{7,6},{8,9},{9,8},{10,11... | collective-permute-start | bytes 3145736 | tf_op jit(solution)/shard_map/ppermute | solution.py:35
where the time goes:
time: 157 us
  waiting for transfers between devices  107 us (68%)
  Pallas kernels  24.4 us (16%)
  starting transfers between devices  17.9 us (11%)
  local copies, waits for them, and re-layouts  6.12 us (4%)
    ppermute x9, waiting for transfers between devices, along_chips(): lax.ppermute(array, 'dp', [(i, (i + by * CORES) % length) for i in range(...  101 us
    ppermute x9, starting transfers between devices, along_chips(): lax.ppermute(array, 'dp', [(i, (i + by * CORES) % length) for i in range(...  16.1 us
    pallas_call x4, Pallas kernels, outer(): call(functools.partial(outer_kernel, arrays, len(before)), 'outer', 2 * a...  6.99 us
    pallas_call x1, Pallas kernels, project(): call(functools.partial(project_kernel, chips, steps), 'project', 4 * chip...  6.53 us
    unnamed x23, local copies, waits for them, and re-layouts  5.36 us
    ppermute x1, waiting for transfers between devices, from_behind(): return lax.ppermute(array, axis, pairs)  5.25 us
    pallas_call x1, Pallas kernels, attend(): call(attend_kernel, 'attend', 4 * tokens * tokens * queries.shape[1], 4 *...  4.48 us
    pallas_call x1, Pallas kernels, norm_backward(): call(functools.partial(backward_kernel, len(cots)), 'norm_backward', 10 *...  3.26 us
  transfers between devices with their start and end apart: 12, of which 9 were waited for; matrix products, arithmetic and copies ran while one was open for 1% of the time, Pallas kernels for 11%

commit v1 on v0

--- a/solution.py
+++ b/solution.py
@@ -283,7 +283,7 @@
     other_weight = swap_cores(kv_weight[0])
     value_cot = attend(queries[0], new_keys[0], context_grad[0], segment_ids)
 
-    after = [rows[by] for by in order[:-1]]
+    after = rows[1:]
     early = normalize(place, new_input[0], new_gain, value_cot, chips, [0] + first, after)
     columns = [early[0]] + [along_chips(block, by) for block, by in zip(early[1:], first)]
 
@@ -298,7 +298,7 @@
     cot_below = from_behind(input_cot, "pipe", -1)
 
     sums = [outer(columns[:-1], kv_width, half, [], jnp.float32, []) for half in range(CORES)]
-    given = outer(columns[-1:], kv_width, 1, [sums[1]], jnp.bfloat16, [cot_below])
+    given = outer(columns[-1:], kv_width, 1, [sums[1]], jnp.bfloat16, [])
     taken = swap_cores(given)
     grad = outer(columns[-1:], kv_width, 0, [sums[0], taken], jnp.float32, [])
     return (cot_below[None], grad[None])

time: 157 us -> 149 us (0.949)
  the two profiles are of different devices: /device:TPU:0 before, /device:TPU:10 now
where the time goes in v1:
time: 149 us; the launch traced here: 147 us
  waiting for transfers between devices  100 us (67%)
  Pallas kernels  24.3 us (16%)
  starting transfers between devices  15.2 us (10%)
  local copies, waits for them, and re-layouts  6.12 us (4%)
    ppermute x9, waiting for transfers between devices, along_chips(): lax.ppermute(array, 'dp', [(i, (i + by * CORES) % length) for i in range(...  99.4 us
    ppermute x9, starting transfers between devices, along_chips(): lax.ppermute(array, 'dp', [(i, (i + by * CORES) % length) for i in range(...  12.7 us
    pallas_call x4, Pallas kernels, outer(): call(functools.partial(outer_kernel, arrays, len(before)), 'outer', 2 * a...  6.99 us
    pallas_call x1, Pallas kernels, project(): call(functools.partial(project_kernel, chips, steps), 'project', 4 * chip...  6.51 us
    unnamed x23, local copies, waits for them, and re-layouts  5.36 us
    pallas_call x1, Pallas kernels, attend(): call(attend_kernel, 'attend', 4 * tokens * tokens * queries.shape[1], 4 *...  4.47 us
    pallas_call x1, Pallas kernels, norm_backward(): call(functools.partial(backward_kernel, len(cots)), 'norm_backward', 10 *...  3.25 us
    pallas_call x2, Pallas kernels, normalize(): call(functools.partial(norm_kernel, chips, ahead), 'norm_forward', 4 * to...  3.09 us
  transfers between devices with their start and end apart: 12, of which 9 were waited for; matrix products, arithmetic and copies ran while one was open for 1% of the time, Pallas kernels for 14%

profile of v1, /device:TPU:10, one launch (start us, length us, event | category | flops | bytes accessed | tf_op | source)
XLA Modules:
  0.0 146.9 jit_solution(9920014291448678986)
XLA Ops:
  0.6 0.0 copy-start
  0.6 0.1 collective-permute-start
  0.7 1.6 %collective-permute-start.3 = (bf16[128,1024]{1,0:T(8,128)(2,1)}, bf16[128,1024]{1,0:T(8,128)(2,1)S(1)}, u32[]{:S(2)}, u32[]{:S(2)}) collective-permute-start(bf16[128,1024]{1,0:T(8,128)(2,1)} %bitcast.23), channel_id=1, source_target_pairs={{0,2},{1,3},{2,4},{3,5},{4,6},{5,7},{6,0},{7,1},{8,10},{9,11},{10,... | collective-permute-start | bytes 786440 | tf_op jit(solution)/shard_map/ppermute | solution.py:30
  2.4 1.2 collective-permute-start.2
  3.6 1.8 %collective-permute-start.1 = (bf16[128,1024]{1,0:T(8,128)(2,1)}, bf16[128,1024]{1,0:T(8,128)(2,1)S(1)}, u32[]{:S(2)}, u32[]{:S(2)}) collective-permute-start(bf16[128,1024]{1,0:T(8,128)(2,1)} %bitcast.25), channel_id=1, source_target_pairs={{0,6},{1,7},{2,0},{3,1},{4,2},{5,3},{6,4},{7,5},{8,14},{9,15},{10,... | collective-permute-start | bytes 786440 | tf_op jit(solution)/shard_map/ppermute | solution.py:30
  5.4 0.8 copy.13.col_seg_ref
  6.2 0.0 copy-start.3
  6.2 1.2 copy-done.3
  7.4 1.2 copy-done.4
  8.6 0.9 copy-done.6
  9.5 0.7 copy-done.8
  10.2 4.5 %attend.1.cot_ref = bf16[128,512]{1,0:T(8,128)(2,1)S(1)} custom-call(bf16[128,4096]{1,0:T(8,128)(2,1)S(1)} %bitcast.17, bf16[128,512]{1,0:T(8,128)(2,1)S(1)} %bitcast.19, bf16[128,4096]{1,0:T(8,128)(2,1)S(1)} %bitcast.18, s32[1,128]{1,0:T(1,128)S(1)} %copy-done.8, s32[128,1]{1,0:T(8,128)S(1)} %copy.13.col_seg_ref), custom_call_target="tpu_custom_call" | custom-call | flops 268435456 | bytes 2097152 | tf_op jit(solution)/shard_map/attend/pallas_call | solution.py:119
  14.7 0.0 copy-start.9
  14.7 0.0 copy-start.10
  14.7 0.1 pad_add_fusion.place_ref
  14.8 5.6 %collective-permute-done.3.rest_2_.rest_3_ = bf16[128,1024]{1,0:T(8,128)(2,1)S(1)} collective-permute-done((bf16[128,1024]{1,0:T(8,128)(2,1)}, bf16[128,1024]{1,0:T(8,128)(2,1)S(1)}, u32[]{:S(2)}, u32[]{:S(2)}) %collective-permute-start.3) | collective-permute-done | bytes 262176 | tf_op jit(solution)/shard_map/ppermute | solution.py:30
  20.4 5.3 %collective-permute-done.2.rest_1_.rest_2_ = bf16[128,1024]{1,0:T(8,128)(2,1)S(1)} collective-permute-done((bf16[128,1024]{1,0:T(8,128)(2,1)}, bf16[128,1024]{1,0:T(8,128)(2,1)S(1)}, u32[]{:S(2)}, u32[]{:S(2)}) %collective-permute-start.2) | collective-permute-done | bytes 262176 | tf_op jit(solution)/shard_map/ppermute | solution.py:30
  25.7 1.7 %collective-permute-done.1.rest_0_.rest_1_ = bf16[128,1024]{1,0:T(8,128)(2,1)S(1)} collective-permute-done((bf16[128,1024]{1,0:T(8,128)(2,1)}, bf16[128,1024]{1,0:T(8,128)(2,1)S(1)}, u32[]{:S(2)}, u32[]{:S(2)}) %collective-permute-start.1) | collective-permute-done | bytes 262176 | tf_op jit(solution)/shard_map/ppermute | solution.py:30
  27.4 1.5 %norm_forward.2 = (bf16[128,2560]{1,0:T(8,128)(2,1)S(1)}, bf16[128,2560]{1,0:T(8,128)(2,1)S(1)}) custom-call(s32[2]{0:T(128)S(1)} %pad_add_fusion.place_ref, bf16[128,8192]{1,0:T(8,128)(2,1)S(1)} %bitcast.13, bf16[1,8192]{1,0:T(2,128)(2,1)S(1)} %copy-done.5, bf16[128,512]{1,0:T(8,128)(2,1)S(1)} %attend.1.cot_ref, ...), custom_call_target="tpu_custom_call" | custom-call | flops 4194304 | bytes 3407872 | tf_op jit(solution)/shard_map/norm_forward/pallas_call | solution.py:75
  28.9 0.1 collective-permute-start.7
  29.0 0.0 collective-permute-done.other_ref
  29.0 0.0 copy-start.2
  29.0 6.5 %project.1 = (bf16[128,2048]{1,0:T(8,128)(2,1)S(1)}, bf16[128,2048]{1,0:T(8,128)(2,1)S(1)}, bf16[128,2048]{1,0:T(8,128)(2,1)S(1)}, bf16[128,2048]{1,0:T(8,128)(2,1)S(1)}) custom-call(bf16[1024,1024]{1,0:T(8,128)(2,1)S(1)} %bitcast.22, bf16[1024,1024]{1,0:T(8,128)(2,1)} %collective-permute-done.other_ref, bf16[128,1024]{1,0:T(8,128)(2,1)S(1)} %bitcast.26, ...), custom_call_target="tpu_custom_call" | custom-call | flops 2147483648 | bytes 7340032 | tf_op jit(solution)/shard_map/project/pallas_call | solution.py:168
  35.6 0.0 copy-start.1
  35.6 0.0 copy-start.7
  35.6 2.2 %collective-permute-start.4 = (bf16[128,2048]{1,0:T(8,128)(2,1)S(1)}, bf16[128,2048]{1,0:T(8,128)(2,1)S(1)}, u32[]{:S(2)}, u32[]{:S(2)}) collective-permute-start(bf16[128,2048]{1,0:T(8,128)(2,1)S(1)} %get-tuple-element.12), channel_id=1, source_target_pairs={{0,2},{1,3},{2,4},{3,5},{4,6},{5,7},{6,0},{7,1},{8,10},{9,11},{10,... | collective-permute-start | bytes 1572872 | tf_op jit(solution)/shard_map/ppermute | solution.py:30
  37.8 0.0 collective-permute-start.6
  37.8 2.2 %collective-permute-start.5 = (bf16[128,2048]{1,0:T(8,128)(2,1)S(1)}, bf16[128,2048]{1,0:T(8,128)(2,1)S(1)}, u32[]{:S(2)}, u32[]{:S(2)}) collective-permute-start(bf16[128,2048]{1,0:T(8,128)(2,1)S(1)} %get-tuple-element.13), channel_id=1, source_target_pairs={{0,4},{1,5},{2,6},{3,7},{4,0},{5,1},{6,2},{7,3},{8,12},{9,13},{10,... | collective-permute-start | bytes 1572872 | tf_op jit(solution)/shard_map/ppermute | solution.py:30
  40.0 17.8 %collective-permute-done.4.rest_0_.rest_1_ = bf16[128,2048]{1,0:T(8,128)(2,1)S(1)} collective-permute-done((bf16[128,2048]{1,0:T(8,128)(2,1)S(1)}, bf16[128,2048]{1,0:T(8,128)(2,1)S(1)}, u32[]{:S(2)}, u32[]{:S(2)}) %collective-permute-start.4) | collective-permute-done | bytes 524320 | tf_op jit(solution)/shard_map/ppermute | solution.py:30
  57.8 10.9 %collective-permute-done.6.rest_1_.rest_3_ = bf16[128,2048]{1,0:T(8,128)(2,1)S(1)} collective-permute-done((bf16[128,2048]{1,0:T(8,128)(2,1)S(1)}, bf16[128,2048]{1,0:T(8,128)(2,1)S(1)}, u32[]{:S(2)}, u32[]{:S(2)}) %collective-permute-start.6) | collective-permute-done | bytes 524320 | tf_op jit(solution)/shard_map/ppermute | solution.py:30
  68.8 1.5 %norm_forward.3 = (bf16[128,2560]{1,0:T(8,128)(2,1)S(1)}, bf16[128,2560]{1,0:T(8,128)(2,1)S(1)}) custom-call(s32[2]{0:T(128)S(1)} %pad_add_fusion.place_ref, bf16[128,8192]{1,0:T(8,128)(2,1)S(1)} %bitcast.14, bf16[1,8192]{1,0:T(2,128)(2,1)S(1)} %copy-done.5, bf16[128,512]{1,0:T(8,128)(2,1)S(1)} %attend.1.cot_ref, ...), custom_call_target="tpu_custom_call" | custom-call | flops 4194304 | bytes 3407872 | tf_op jit(solution)/shard_map/norm_forward/pallas_call | solution.py:75
  70.3 0.0 collective-permute-done.7.rest_5_.refs_1_.refs_4_
  70.3 18.1 %collective-permute-done.5.rest_2_ = bf16[128,2048]{1,0:T(8,128)(2,1)S(1)} collective-permute-done((bf16[128,2048]{1,0:T(8,128)(2,1)S(1)}, bf16[128,2048]{1,0:T(8,128)(2,1)S(1)}, u32[]{:S(2)}, u32[]{:S(2)}) %collective-permute-start.5) | collective-permute-done | bytes 524320 | tf_op jit(solution)/shard_map/ppermute | solution.py:30
  88.4 0.0 copy-done.1
  88.4 3.3 %norm_backward.1 = bf16[128,8192]{1,0:T(8,128)(2,1)S(1)} custom-call(s32[2]{0:T(128)S(1)} %pad_add_fusion.place_ref, bf16[128,8192]{1,0:T(8,128)(2,1)S(1)} %bitcast.15, bf16[1,8192]{1,0:T(2,128)(2,1)S(1)} %copy-done.7, bf16[128,8192]{1,0:T(8,128)(2,1)S(1)} %bitcast.16, bf16[128,2048]{1,0:T(8,128)(2,1)S(1)} %get-tuple-element.11.rest_0_, ...), custom_call_target="tpu_custom_call" | custom-call | flops 10485760 | bytes 8388608 | tf_op jit(solution)/shard_map/norm_backward/pallas_call | solution.py:213
  91.7 2.4 %collective-permute-start.8 = (bf16[128,8192]{1,0:T(8,128)(2,1)S(1)}, bf16[128,8192]{1,0:T(8,128)(2,1)S(1)}, u32[]{:S(2)}, u32[]{:S(2)}) collective-permute-start(bf16[128,8192]{1,0:T(8,128)(2,1)S(1)} %norm_backward.1), channel_id=1, source_target_pairs={{8,0},{16,8},{24,16},{9,1},{17,9},{25,17},{10,2},{18,10},{26,18},{... | collective-permute-start | bytes 6291464 | tf_op jit(solution)/shard_map/ppermute | solution.py:25
  94.1 3.2 %collective-permute-start.10 = (bf16[128,2560]{1,0:T(8,128)(2,1)S(1)}, bf16[128,2560]{1,0:T(8,128)(2,1)S(1)}, u32[]{:S(2)}, u32[]{:S(2)}) collective-permute-start(bf16[128,2560]{1,0:T(8,128)(2,1)S(1)} %get-tuple-element.15.rest_4_), channel_id=1, source_target_pairs={{0,6},{1,7},{2,0},{3,1},{4,2},{5,3},{6,4},{7,5},{8,14},{9,15},{10,... | collective-permute-start | bytes 1966088 | tf_op jit(solution)/shard_map/ppermute | solution.py:30
  97.3 0.3 collective-permute-start.9
  97.7 28.2 %collective-permute-done.10.refs_2_.refs_5_ = bf16[128,2560]{1,0:T(8,128)(2,1)S(1)} collective-permute-done((bf16[128,2560]{1,0:T(8,128)(2,1)S(1)}, bf16[128,2560]{1,0:T(8,128)(2,1)S(1)}, u32[]{:S(2)}, u32[]{:S(2)}) %collective-permute-start.10) | collective-permute-done | bytes 655392 | tf_op jit(solution)/shard_map/ppermute | solution.py:30
  125.9 1.7 %outer.5.refs_2_ = f32[1024,512]{1,0:T(8,128)S(1)} custom-call(bf16[128,2560]{1,0:T(8,128)(2,1)S(1)} %get-tuple-element.10.rest_4_.refs_0_.refs_3_, bf16[128,2560]{1,0:T(8,128)(2,1)S(1)} %collective-permute-done.7.rest_5_.refs_1_.refs_4_, bf16[128,2560]{1,0:T(8,128)(2,1)S(1)} %collective-permute-done.10.refs_2_.refs_5_, ...), custom_call_target="tpu_custom_call" | custom-call | flops 402653184 | bytes 2883584 | tf_op jit(solution)/shard_map/outer/pallas_call | solution.py:249
  127.6 11.7 %collective-permute-done.9.refs_0_.refs_1_ = bf16[128,2560]{1,0:T(8,128)(2,1)S(1)} collective-permute-done((bf16[128,2560]{1,0:T(8,128)(2,1)S(1)}, bf16[128,2560]{1,0:T(8,128)(2,1)S(1)}, u32[]{:S(2)}, u32[]{:S(2)}) %collective-permute-start.9) | collective-permute-done | bytes 655392 | tf_op jit(solution)/shard_map/ppermute | solution.py:30
  139.3 1.1 outer.6
  140.4 0.1 collective-permute-start.11
  140.5 1.8 %outer.4.refs_2_ = f32[1024,512]{1,0:T(8,128)S(1)} custom-call(bf16[128,2560]{1,0:T(8,128)(2,1)S(1)} %get-tuple-element.10.rest_4_.refs_0_.refs_3_, bf16[128,2560]{1,0:T(8,128)(2,1)S(1)} %collective-permute-done.7.rest_5_.refs_1_.refs_4_, bf16[128,2560]{1,0:T(8,128)(2,1)S(1)} %collective-permute-done.10.refs_2_.refs_5_, ...), custom_call_target="tpu_custom_call" | custom-call | flops 402653184 | bytes 2883584 | tf_op jit(solution)/shard_map/outer/pallas_call | solution.py:249
  142.3 0.9 collective-permute-done.11.refs_3_
  143.2 2.4 %outer.7 = f32[1024,512]{1,0:T(8,128)} custom-call(bf16[128,2560]{1,0:T(8,128)(2,1)S(1)} %collective-permute-done.9.refs_0_.refs_1_, bf16[128,2560]{1,0:T(8,128)(2,1)S(1)} %collective-permute-done.9.refs_0_.refs_1_, f32[1024,512]{1,0:T(8,128)S(1)} %outer.4.refs_2_, bf16[1024,512]{1,0:T(8,128)(2,1)S(1)} %collective-permute-done.11.refs_3_), custom_call_target="tpu_custom_call" | custom-call | flops 134217728 | bytes 2359296 | tf_op jit(solution)/shard_map/outer/pallas_call | solution.py:249
  145.5 0.0 collective-permute-done.8
  145.6 1.3 copy.15
  (10 shorter events, 0.0 us)
Async XLA Ops:
  0.6 26.8 %copy-start = (bf16[1,128,8192]{2,1,0:T(8,128)(2,1)S(1)}, bf16[1,128,8192]{2,1,0:T(8,128)(2,1)}, u32[]{:S(2)}) copy-start(bf16[1,128,8192]{2,1,0:T(8,128)(2,1)} %param.11) | copy-start | bytes 6291460
  0.6 28.4 %collective-permute-start = (bf16[1024,1024]{1,0:T(8,128)(2,1)}, bf16[1024,1024]{1,0:T(8,128)(2,1)}, u32[]{:S(2)}, u32[]{:S(2)}) collective-permute-start(bf16[1024,1024]{1,0:T(8,128)(2,1)} %bitcast.21), channel_id=1, source_target_pairs={{0,1},{1,0},{2,3},{3,2},{4,5},{5,4},{6,7},{7,6},{8,9},{9,8},{10,11... | collective-permute-start | bytes 6291464 | tf_op jit(solution)/shard_map/ppermute | solution.py:35
  0.7 19.7 %collective-permute-start.3 = (bf16[128,1024]{1,0:T(8,128)(2,1)}, bf16[128,1024]{1,0:T(8,128)(2,1)S(1)}, u32[]{:S(2)}, u32[]{:S(2)}) collective-permute-start(bf16[128,1024]{1,0:T(8,128)(2,1)} %bitcast.23), channel_id=1, source_target_pairs={{0,2},{1,3},{2,4},{3,5},{4,6},{5,7},{6,0},{7,1},{8,10},{9,11},{10,... | collective-permute-start | bytes 786440 | tf_op jit(solution)/shard_map/ppermute | solution.py:30
  2.4 23.3 %collective-permute-start.2 = (bf16[128,1024]{1,0:T(8,128)(2,1)}, bf16[128,1024]{1,0:T(8,128)(2,1)S(1)}, u32[]{:S(2)}, u32[]{:S(2)}) collective-permute-start(bf16[128,1024]{1,0:T(8,128)(2,1)} %bitcast.24), channel_id=1, source_target_pairs={{0,4},{1,5},{2,6},{3,7},{4,0},{5,1},{6,2},{7,3},{8,12},{9,13},{10,... | collective-permute-start | bytes 786440 | tf_op jit(solution)/shard_map/ppermute | solution.py:30
  3.6 23.8 %collective-permute-start.1 = (bf16[128,1024]{1,0:T(8,128)(2,1)}, bf16[128,1024]{1,0:T(8,128)(2,1)S(1)}, u32[]{:S(2)}, u32[]{:S(2)}) collective-permute-start(bf16[128,1024]{1,0:T(8,128)(2,1)} %bitcast.25), channel_id=1, source_target_pairs={{0,6},{1,7},{2,0},{3,1},{4,2},{5,3},{6,4},{7,5},{8,14},{9,15},{10,... | collective-permute-start | bytes 786440 | tf_op jit(solution)/shard_map/ppermute | solution.py:30
  6.2 1.2 copy-start.3
  7.4 1.2 copy-start.4
  8.6 0.9 copy-start.6
  9.5 0.7 copy-start.8
  10.2 17.2 %copy-start.5 = (bf16[1,8192]{1,0:T(2,128)(2,1)S(1)}, bf16[1,8192]{1,0:T(2,128)(2,1)}, u32[]{:S(2)}) copy-start(bf16[1,8192]{1,0:T(2,128)(2,1)} %gain_ref.4) | copy-start | bytes 49156
  14.7 14.4 %copy-start.9 = (bf16[1,1024,1024]{2,1,0:T(8,128)(2,1)S(1)}, bf16[1,1024,1024]{2,1,0:T(8,128)(2,1)}, u32[]{:S(2)}) copy-start(bf16[1,1024,1024]{2,1,0:T(8,128)(2,1)} %param.21) | copy-start | bytes 6291460
  14.7 14.4 %copy-start.10 = (bf16[1,128,1024]{2,1,0:T(8,128)(2,1)S(1)}, bf16[1,128,1024]{2,1,0:T(8,128)(2,1)}, u32[]{:S(2)}) copy-start(bf16[1,128,1024]{2,1,0:T(8,128)(2,1)} %param.20) | copy-start | bytes 786436
  28.9 41.4 %collective-permute-start.7 = (bf16[128,2560]{1,0:T(8,128)(2,1)S(1)}, bf16[128,2560]{1,0:T(8,128)(2,1)S(1)}, u32[]{:S(2)}, u32[]{:S(2)}) collective-permute-start(bf16[128,2560]{1,0:T(8,128)(2,1)S(1)} %get-tuple-element.16), channel_id=1, source_target_pairs={{0,2},{1,3},{2,4},{3,5},{4,6},{5,7},{6,0},{7,1},{8,10},{9,11},{10,... | collective-permute-start | bytes 1966088 | tf_op jit(solution)/shard_map/ppermute | solution.py:30
  29.0 59.4 %copy-start.2 = (bf16[1,128,8192]{2,1,0:T(8,128)(2,1)S(1)}, bf16[1,128,8192]{2,1,0:T(8,128)(2,1)}, u32[]{:S(2)}) copy-start(bf16[1,128,8192]{2,1,0:T(8,128)(2,1)} %param.19) | copy-start | bytes 6291460
  35.6 52.8 %copy-start.1 = (bf16[1,128,8192]{2,1,0:T(8,128)(2,1)S(1)}, bf16[1,128,8192]{2,1,0:T(8,128)(2,1)}, u32[]{:S(2)}) copy-start(bf16[1,128,8192]{2,1,0:T(8,128)(2,1)} %param.17) | copy-start | bytes 6291460
  35.6 52.8 %copy-start.7 = (bf16[1,8192]{1,0:T(2,128)(2,1)S(1)}, bf16[1,8192]{1,0:T(2,128)(2,1)}, u32[]{:S(2)}) copy-start(bf16[1,8192]{1,0:T(2,128)(2,1)} %gain_ref.5) | copy-start | bytes 49156
  35.6 22.2 %collective-permute-start.4 = (bf16[128,2048]{1,0:T(8,128)(2,1)S(1)}, bf16[128,2048]{1,0:T(8,128)(2,1)S(1)}, u32[]{:S(2)}, u32[]{:S(2)}) collective-permute-start(bf16[128,2048]{1,0:T(8,128)(2,1)S(1)} %get-tuple-element.12), channel_id=1, source_target_pairs={{0,2},{1,3},{2,4},{3,5},{4,6},{5,7},{6,0},{7,1},{8,10},{9,11},{10,... | collective-permute-start | bytes 1572872 | tf_op jit(solution)/shard_map/ppermute | solution.py:30
  37.8 31.0 %collective-permute-start.6 = (bf16[128,2048]{1,0:T(8,128)(2,1)S(1)}, bf16[128,2048]{1,0:T(8,128)(2,1)S(1)}, u32[]{:S(2)}, u32[]{:S(2)}) collective-permute-start(bf16[128,2048]{1,0:T(8,128)(2,1)S(1)} %get-tuple-element.14), channel_id=1, source_target_pairs={{0,6},{1,7},{2,0},{3,1},{4,2},{5,3},{6,4},{7,5},{8,14},{9,15},{10,... | collective-permute-start | bytes 1572872 | tf_op jit(solution)/shard_map/ppermute | solution.py:30
  37.8 50.6 %collective-permute-start.5 = (bf16[128,2048]{1,0:T(8,128)(2,1)S(1)}, bf16[128,2048]{1,0:T(8,128)(2,1)S(1)}, u32[]{:S(2)}, u32[]{:S(2)}) collective-permute-start(bf16[128,2048]{1,0:T(8,128)(2,1)S(1)} %get-tuple-element.13), channel_id=1, source_target_pairs={{0,4},{1,5},{2,6},{3,7},{4,0},{5,1},{6,2},{7,3},{8,12},{9,13},{10,... | collective-permute-start | bytes 1572872 | tf_op jit(solution)/shard_map/ppermute | solution.py:30
  91.7 53.9 %collective-permute-start.8 = (bf16[128,8192]{1,0:T(8,128)(2,1)S(1)}, bf16[128,8192]{1,0:T(8,128)(2,1)S(1)}, u32[]{:S(2)}, u32[]{:S(2)}) collective-permute-start(bf16[128,8192]{1,0:T(8,128)(2,1)S(1)} %norm_backward.1), channel_id=1, source_target_pairs={{8,0},{16,8},{24,16},{9,1},{17,9},{25,17},{10,2},{18,10},{26,18},{... | collective-permute-start | bytes 6291464 | tf_op jit(solution)/shard_map/ppermute | solution.py:25
  94.1 31.8 %collective-permute-start.10 = (bf16[128,2560]{1,0:T(8,128)(2,1)S(1)}, bf16[128,2560]{1,0:T(8,128)(2,1)S(1)}, u32[]{:S(2)}, u32[]{:S(2)}) collective-permute-start(bf16[128,2560]{1,0:T(8,128)(2,1)S(1)} %get-tuple-element.15.rest_4_), channel_id=1, source_target_pairs={{0,6},{1,7},{2,0},{3,1},{4,2},{5,3},{6,4},{7,5},{8,14},{9,15},{10,... | collective-permute-start | bytes 1966088 | tf_op jit(solution)/shard_map/ppermute | solution.py:30
  97.3 42.0 %collective-permute-start.9 = (bf16[128,2560]{1,0:T(8,128)(2,1)S(1)}, bf16[128,2560]{1,0:T(8,128)(2,1)S(1)}, u32[]{:S(2)}, u32[]{:S(2)}) collective-permute-start(bf16[128,2560]{1,0:T(8,128)(2,1)S(1)} %get-tuple-element.17), channel_id=1, source_target_pairs={{0,4},{1,5},{2,6},{3,7},{4,0},{5,1},{6,2},{7,3},{8,12},{9,13},{10,... | collective-permute-start | bytes 1966088 | tf_op jit(solution)/shard_map/ppermute | solution.py:30
  140.4 2.7 %collective-permute-start.11 = (bf16[1024,512]{1,0:T(8,128)(2,1)S(1)}, bf16[1024,512]{1,0:T(8,128)(2,1)S(1)}, u32[]{:S(2)}, u32[]{:S(2)}) collective-permute-start(bf16[1024,512]{1,0:T(8,128)(2,1)S(1)} %outer.6), channel_id=1, source_target_pairs={{0,1},{1,0},{2,3},{3,2},{4,5},{5,4},{6,7},{7,6},{8,9},{9,8},{10,11... | collective-permute-start | bytes 3145736 | tf_op jit(solution)/shard_map/ppermute | solution.py:35
